TPU v7x, 32 devices: a whole 2x2x4 slice. The times are simulated.
32 devices in a mesh: grp: 2 (over y), gx: 16 (over z, x, core).
Axes of the slice: x: 2, y: 2, z: 4, core: 2. Of those that a mesh axis runs over, the one named last changes fastest.
Arguments:
- fields: float32 [32, 32, 256, 256], P('grp', 'gx'), parts along dimension 0, may hold values from -400 to 400
- factor_x: float32 [64, 96], P('grp'), parts along dimension 0, may hold values from -1 to 1
- factor_y: float32 [512, 96], P('grp'), parts along dimension 0, may hold values from -0.375 to 0.375
- factor_z: float32 [512, 96], P('grp'), parts along dimension 0, may hold values from -0.375 to 0.375
- factor_var: float32 [32, 8], P('grp'), parts along dimension 0, may hold values from -1.5 to 1.5
Outputs:
- core_tensor: float32 [18432, 8, 96], P(('grp', 'gx')), parts along dimension 0
- gram_vars: float32 [32, 16], P('grp'), parts along dimension 0
- gram_y: float32 [512, 256], P('grp'), parts along dimension 0
- gram_z: float32 [512, 256], P('grp'), parts along dimension 0
There are 2 independent parts, one for each index of `grp`. A program takes and returns all parts, laid end to end along the dimension named above; each array names one. Nothing has to cross between parts.
All inputs are finite; a program needn't handle non-finite values.
Results may differ from a plain program's by a relative error of at most 0.000071.
Values sent between devices are 32-bit elements; how exact they have to be, the bound alone decides.
A program may use at most 64 MiB of HBM per device.

v0:
```python
import jax
import jax.numpy as jnp
from jax import lax
from jax.experimental import pallas as pl
from jax.experimental.pallas import tpu as pltpu
from jax.sharding import PartitionSpec as P

F32 = jnp.float32
BF16 = jnp.bfloat16
MESH = pl.DeviceIdType.MESH


def plain(fields, factor_x, factor_y, factor_z, factor_var):
    highest = lax.Precision.HIGHEST
    devices = lax.axis_size("gx")
    slab_rows = fields.shape[1]
    total_x = slab_rows * devices
    var_count = fields.shape[0]
    cells_y = fields.shape[2]
    cells_z = fields.shape[3]
    local_vars = jnp.einsum("vxyz,wxyz->vw", fields, fields, precision=highest)
    local_y = jnp.einsum("vxyz,vxuz->yu", fields, fields, precision=highest)
    flat = fields.reshape(-1, cells_z)
    local_z = jnp.dot(flat.T, flat, precision=highest, preferred_element_type=jnp.float32)
    summed_vars, summed_y, summed_z = lax.psum((local_vars, local_y, local_z), "gx")
    gram_vars = summed_vars / float(total_x * cells_y * cells_z)
    gram_y = summed_y / float(var_count * total_x * cells_z)
    gram_z = summed_z / float(var_count * total_x * cells_y)
    reduced_var = jnp.einsum("va,vxyz->axyz", factor_var, fields, precision=highest)
    reduced_z = jnp.einsum("axyz,zk->axyk", reduced_var, factor_z, precision=highest)
    reduced_y = jnp.einsum("axyk,yj->xajk", reduced_z, factor_y, precision=highest)
    comp_count = reduced_y.shape[1]
    projected = reduced_y.reshape(slab_rows, comp_count, reduced_y.shape[2] * reduced_y.shape[3])
    core_tensor = jnp.einsum(
        "xak,xr->kar",
        lax.all_to_all(projected, "gx", split_axis=2, concat_axis=0, tiled=True),
        factor_x,
        precision=highest,
    )
    return (core_tensor, gram_vars, gram_y, gram_z)


N = 16
V = 16
A = 8
S = 2
C = 256
R = 96
KP = 128
JD = R // N
CH = JD * S * A
GROUP = 4


def split(value):
    high = value.astype(BF16)
    return high, (value - high.astype(F32)).astype(BF16)


def dot(a, b):
    return jnp.dot(a, b, preferred_element_type=F32)


def kernel(f_ref, fx_ref, fy_ref, fz_ref, fv_ref, core_ref, gv_out, gy_out, gz_out,
           h_ref, l_ref, zhl, yhl, pad, w_ref, p_ref, r_ref, gy_acc, gz_acc, gv_acc,
           gram, half, quarter, eighth, recv_a, recv_b, recv_c, gv_all,
           s_core, r_core, s_gv, r_gv, s_a, r_a, s_b, r_b, s_c, r_c,
           s_cg, r_cg, s_bg, r_bg, s_ag, r_ag):
    me = lax.axis_index("gx")

    barrier = pltpu.get_barrier_semaphore()
    for off in range(1, N):
        pl.semaphore_signal(barrier, inc=1, device_id={"gx": lax.rem(me + off, N)}, device_id_type=MESH)

    def remote(src, dst, ssem, rsem, peer):
        return pltpu.make_async_remote_copy(
            src_ref=src, dst_ref=dst, send_sem=ssem, recv_sem=rsem,
            device_id={"gx": peer}, device_id_type=MESH)

    pad[...] = jnp.zeros((C, KP), F32)
    pad[:, 0:R] = fz_ref[...]
    z_high, z_low = split(pad[...])
    zhl[:, 0:KP] = z_high
    zhl[:, KP:2 * KP] = z_low
    pad[:, 0:R] = fy_ref[...]
    y_high, y_low = split(pad[...].T[0:R, :])
    yhl[0:R, :] = y_high
    yhl[R:2 * R, :] = y_low

    def project(i, carry):
        x = i // (V // GROUP)
        first = lax.rem(i, V // GROUP) * GROUP
        for u in range(GROUP):
            v = first + u
            high, low = split(f_ref[v, x])
            h_ref[v, x] = high
            l_ref[v, x] = low
            o = dot(yhl[...], jnp.concatenate([high, low], axis=1))
            along_y = o[0:R, 0:C] + (o[0:R, C:] + o[R:, 0:C])
            u_high, u_low = split(along_y)
            q = dot(jnp.concatenate([u_high, u_low], axis=0), zhl[...])
            w_ref[x * V + v] = q[0:R, 0:KP] + (q[0:R, KP:] + q[R:, 0:KP])
        return carry

    lax.fori_loop(0, S * V // GROUP, project, 0)

    for x in range(S):
        for a in range(A):
            total = fv_ref[0, a] * w_ref[x * V]
            for v in range(1, V):
                total = total + fv_ref[v, a] * w_ref[x * V + v]
            p_ref[pl.ds(x * A + a, R, stride=S * A), :] = total

    pl.semaphore_wait(barrier, N - 1)

    def chunk(index):
        return pl.ds(pl.multiple_of(index * CH, CH), CH)

    def core_copy(off):
        peer = lax.rem(me + off, N)
        return remote(p_ref.at[chunk(peer)], r_ref.at[chunk(me)], s_core.at[off], r_core.at[off], peer)

    for off in range(1, N):
        core_copy(off).start()
    r_ref[chunk(me), :] = p_ref[chunk(me), :]

    gy_acc[...] = jnp.zeros((2 * C, C), F32)
    gz_acc[...] = jnp.zeros((C, 2 * C), F32)
    gv_acc[...] = jnp.zeros((2 * C, C), F32)

    def grams(i, carry):
        x = i // (V // GROUP)
        first = lax.rem(i, V // GROUP) * GROUP
        highs = [h_ref[first + u, x] for u in range(GROUP)]
        lows = [l_ref[first + u, x] for u in range(GROUP)]
        turned = [h.T for h in highs]
        both = jnp.concatenate([jnp.concatenate(highs, axis=1), jnp.concatenate(lows, axis=1)], axis=0)
        gy_acc[...] += dot(both, jnp.concatenate(turned, axis=0))
        wide = jnp.concatenate([jnp.concatenate(highs, axis=0), jnp.concatenate(lows, axis=0)], axis=1)
        gz_acc[...] += dot(jnp.concatenate(turned, axis=1), wide)
        rows = [pl.ds(pl.multiple_of((first + u) * 16, 16), 16) for u in range(GROUP)]
        vh = jnp.concatenate([h_ref[:, x, r, :].reshape(C, C) for r in rows], axis=1)
        vl = jnp.concatenate([l_ref[:, x, r, :].reshape(C, C) for r in rows], axis=1)
        gv_acc[...] += lax.dot_general(
            jnp.concatenate([vh, vl], axis=0), vh, (((1,), (1,)), ((), ())), preferred_element_type=F32)
        return carry

    lax.fori_loop(0, S * V // GROUP, grams, 0)

    gram[0:C, :] = gy_acc[0:C, :] + (gy_acc[C:, :] + gy_acc[C:, :].T)
    gram[C:2 * C, :] = gz_acc[:, 0:C] + (gz_acc[:, C:] + gz_acc[:, C:].T)

    core = lax.rem(me, 2)
    xx = lax.rem(me // 2, 2)
    zz = me // 4
    pair = me + 1 - 2 * core
    xpair = me + 2 - 4 * xx

    def rows(start, size):
        return pl.ds(pl.multiple_of(start, size), size)

    copy_a = remote(gram.at[rows((1 - core) * C, C)], recv_a, s_a, r_a, pair)
    copy_a.start()

    row = lax.broadcasted_iota(jnp.int32, (C, C), 0)
    col = lax.broadcasted_iota(jnp.int32, (C, C), 1)
    whole = gv_acc[0:C, :] + (gv_acc[C:, :] + gv_acc[C:, :].T)
    kept = jnp.where(lax.rem(row, 16) == lax.rem(col, 16), whole, 0.0)
    pick_col = (lax.broadcasted_iota(jnp.int32, (C, KP), 0) // 16
                == lax.broadcasted_iota(jnp.int32, (C, KP), 1)).astype(F32)
    pick_row = (lax.broadcasted_iota(jnp.int32, (V, C), 1) // 16
                == lax.broadcasted_iota(jnp.int32, (V, C), 0)).astype(F32)
    highest = lax.Precision.HIGHEST
    by_col = jnp.dot(kept, pick_col, precision=highest, preferred_element_type=F32)
    gv_all[me] = jnp.dot(pick_row, by_col, precision=highest, preferred_element_type=F32)

    def gv_copy(off):
        return remote(gv_all.at[me], gv_all.at[me], s_gv.at[off], r_gv.at[off], lax.rem(me + off, N))

    for off in range(1, N):
        gv_copy(off).start()

    copy_a.wait()
    half[...] = gram[rows(core * C, C), :] + recv_a[...]
    copy_b = remote(half.at[rows((1 - xx) * 128, 128)], recv_b, s_b, r_b, xpair)
    copy_b.start()
    copy_b.wait()
    quarter[...] = half[rows(xx * 128, 128), :] + recv_b[...]

    def zpeer(off):
        return lax.rem(zz + off, 4)

    def c_copy(off):
        return remote(quarter.at[rows(zpeer(off) * 32, 32)], recv_c.at[off - 1],
                      s_c.at[off - 1], r_c.at[off - 1], zpeer(off) * 4 + lax.rem(me, 4))

    for off in range(1, 4):
        c_copy(off).start()
    for off in range(1, 4):
        c_copy(off).wait()
    mine = quarter[rows(zz * 32, 32), :] + (recv_c[0] + (recv_c[1] + recv_c[2]))
    scale = 1.0 / float(V * S * N * C)
    at = core * C + xx * 128 + zz * 32
    eighth[rows(at, 32), :] = mine * scale

    def cg_copy(off):
        return remote(eighth.at[rows(at, 32)], eighth.at[rows(at, 32)],
                      s_cg.at[off - 1], r_cg.at[off - 1], zpeer(off) * 4 + lax.rem(me, 4))

    for off in range(1, 4):
        cg_copy(off).start()
    for off in range(1, 4):
        cg_copy(off).wait()
    at_b = core * C + xx * 128
    copy_bg = remote(eighth.at[rows(at_b, 128)], eighth.at[rows(at_b, 128)], s_bg, r_bg, xpair)
    copy_bg.start()
    copy_bg.wait()
    at_a = core * C
    copy_ag = remote(eighth.at[rows(at_a, C)], eighth.at[rows(at_a, C)], s_ag, r_ag, pair)
    copy_ag.start()

    for off in range(1, N):
        core_copy(off).wait()
    fx_high, fx_low = split(jnp.concatenate(
        [fx_ref[pl.ds(x, N, stride=S), :] for x in range(S)], axis=0))
    weights = jnp.concatenate([fx_high, fx_high, fx_low], axis=0)
    for j in range(JD):
        for a in range(A):
            slab = jnp.concatenate(
                [r_ref[pl.ds(j * S * A + x * A + a, N, stride=CH), :] for x in range(S)], axis=0)
            high, low = split(slab)
            left = jnp.concatenate([high, low, high], axis=0)
            o = lax.dot_general(left, weights, (((0,), (0,)), ((), ())), preferred_element_type=F32)
            core_ref[pl.ds(j * R * A + a, R, stride=A), :] = o[0:R, :]

    for off in range(1, N):
        gv_copy(off).wait()
    total = gv_all[0]
    for d in range(1, N):
        total = total + gv_all[d]
    gv_out[...] = total[:, 0:V] * (1.0 / float(S * N * C * C))
    copy_ag.wait()
    gy_out[...] = eighth[0:C, :]
    gz_out[...] = eighth[C:2 * C, :]


def fused(fields, factor_x, factor_y, factor_z, factor_var):
    vmem = pl.BlockSpec(memory_space=pltpu.VMEM)
    dma = pltpu.SemaphoreType.DMA
    core, gv, gy, gz = pl.pallas_call(
        kernel,
        out_shape=(
            jax.ShapeDtypeStruct((JD * R * A, R), F32),
            jax.ShapeDtypeStruct((V, V), F32),
            jax.ShapeDtypeStruct((C, C), F32),
            jax.ShapeDtypeStruct((C, C), F32),
        ),
        in_specs=[vmem, vmem, vmem, vmem, pl.BlockSpec(memory_space=pltpu.SMEM)],
        out_specs=(vmem, vmem, vmem, vmem),
        scratch_shapes=[
            pltpu.VMEM((V, S, C, C), BF16), pltpu.VMEM((V, S, C, C), BF16),
            pltpu.VMEM((C, 2 * KP), BF16), pltpu.VMEM((2 * R, C), BF16), pltpu.VMEM((C, KP), F32),
            pltpu.VMEM((S * V, R, KP), F32),
            pltpu.VMEM((R * S * A, KP), F32), pltpu.VMEM((N * CH, KP), F32),
            pltpu.VMEM((2 * C, C), F32), pltpu.VMEM((C, 2 * C), F32), pltpu.VMEM((2 * C, C), F32),
            pltpu.VMEM((2 * C, C), F32), pltpu.VMEM((C, C), F32), pltpu.VMEM((128, C), F32),
            pltpu.VMEM((2 * C, C), F32),
            pltpu.VMEM((C, C), F32), pltpu.VMEM((128, C), F32), pltpu.VMEM((3, 32, C), F32),
            pltpu.VMEM((N, V, KP), F32),
            dma((N,)), dma((N,)), dma((N,)), dma((N,)),
            dma, dma, dma, dma, dma((3,)), dma((3,)),
            dma((3,)), dma((3,)), dma, dma, dma, dma,
        ],
        compiler_params=pltpu.CompilerParams(
            collective_id=0, has_side_effects=True, vmem_limit_bytes=56 * 1024 * 1024),
        name="fused",
    )(fields, factor_x, factor_y, factor_z, factor_var)
    return core.reshape(JD * R, A, R), gv, gy, gz


def local(fields, factor_x, factor_y, factor_z, factor_var):
    sizes = (fields.shape, factor_x.shape, factor_y.shape, factor_z.shape, factor_var.shape)
    served = ((V, S, C, C), (S * N, R), (C, R), (C, R), (V, A))
    if lax.axis_size("gx") == N and sizes == served:
        return fused(fields, factor_x, factor_y, factor_z, factor_var)
    return plain(fields, factor_x, factor_y, factor_z, factor_var)


def solution(mesh):
    in_specs = (
        P("grp", "gx", None, None),
        P("grp", None),
        P("grp", None),
        P("grp", None),
        P("grp", None),
    )
    out_specs = (P(("grp", "gx"), None, None), P("grp", None), P("grp", None), P("grp", None))
    return jax.shard_map(local, mesh=mesh, in_specs=in_specs, out_specs=out_specs, check_vma=False)
```

profile of v0, /device:TPU:0, one launch (start us, length us, event | category | flops | bytes accessed | tf_op | source)
XLA Modules:
  0.0 61.9 jit_solution(2542604127181297646)
XLA Ops:
  0.6 1.4 %copy.11.fv_ref = f32[16,8]{1,0:T(8,128)} copy(f32[16,8]{0,1:T(8,128)} %param.9) | data formatting | bytes 1024 | tf_op args[4]
  2.0 1.6 %copy.9.fy_ref = f32[256,96]{1,0:T(8,128)} copy(f32[256,96]{0,1:T(8,128)} %param.7) | data formatting | bytes 196608 | tf_op args[2]
  3.6 1.6 %copy.10.fz_ref = f32[256,96]{1,0:T(8,128)} copy(f32[256,96]{0,1:T(8,128)} %param.8) | data formatting | bytes 196608 | tf_op args[3]
  5.3 51.3 %fused.1 = (f32[4608,96]{1,0:T(8,128)}, f32[16,16]{1,0:T(8,128)}, f32[256,256]{1,0:T(8,128)}, f32[256,256]{1,0:T(8,128)}) custom-call(f32[16,2,256,256]{3,2,1,0:T(8,128)} %f_ref.1, f32[32,96]{1,0:T(8,128)} %fx_ref.1, f32[256,96]{1,0:T(8,128)} %copy.9.fy_ref, f32[256,96]{1,0:T(8,128)} %copy.10.fz_ref, f32[16,8]{1,0:T(8,128)} %copy.11.fv_ref), custom_call_target="tpu_custom_call" | custom-call | tf_op jit(solution)/shard_map/fused/pallas_call | solution.py:250
  56.6 0.0 copy-start.2
  56.6 0.0 copy-start.1
  56.6 0.0 copy-start
  56.6 3.3 %copy.12 = f32[576,8,96]{0,2,1:T(8,128)} copy(f32[576,8,96]{2,1,0:T(8,128)} %bitcast.1) | data formatting | bytes 3538944
  59.9 0.0 copy-done.2
  59.9 0.6 copy.16
  60.5 0.0 copy-done.1
  60.5 0.7 %copy.17 = f32[256,256]{1,0:T(8,128)} copy(f32[256,256]{1,0:T(8,128)S(1)} %copy-done.1) | data formatting | bytes 524288
  61.2 0.0 copy-done
  61.2 0.7 %copy.18 = f32[256,256]{1,0:T(8,128)} copy(f32[256,256]{1,0:T(8,128)S(1)} %copy-done) | data formatting | bytes 524288
Async XLA Ops:
  56.6 3.3 %copy-start.2 = (f32[16,16]{1,0:T(8,128)S(1)}, f32[16,16]{1,0:T(8,128)}, u32[]{:S(2)}) copy-start(f32[16,16]{1,0:T(8,128)} %get-tuple-element.21) | copy-start | bytes 3076
  56.6 3.9 %copy-start.1 = (f32[256,256]{1,0:T(8,128)S(1)}, f32[256,256]{1,0:T(8,128)}, u32[]{:S(2)}) copy-start(f32[256,256]{1,0:T(8,128)} %get-tuple-element.22) | copy-start | bytes 786436
  56.6 4.6 %copy-start = (f32[256,256]{1,0:T(8,128)S(1)}, f32[256,256]{1,0:T(8,128)}, u32[]{:S(2)}) copy-start(f32[256,256]{1,0:T(8,128)} %get-tuple-element.23) | copy-start | bytes 786436
where the time goes:
time: 62.2 us; the launch traced here: 61.9 us
  Pallas kernels  51.3 us (82%)
  local copies, waits for them, and re-layouts  9.96 us (16%)
  between operations  0.67 us (1%)
    pallas_call x1, Pallas kernels, fused(): pl.pallas_call(kernel, out_shape=(jax.ShapeDtypeStruct((JD * R * A, R), F...  51.3 us
    unnamed x13, local copies, waits for them, and re-layouts  9.96 us

commit v1 on v0

v1 whole, which is shorter than its diff:
```python
import jax
import jax.numpy as jnp
from jax import lax
from jax.experimental import pallas as pl
from jax.experimental.pallas import tpu as pltpu
from jax.sharding import PartitionSpec as P

F32 = jnp.float32
BF16 = jnp.bfloat16
MESH = pl.DeviceIdType.MESH


def plain(fields, factor_x, factor_y, factor_z, factor_var):
    highest = lax.Precision.HIGHEST
    devices = lax.axis_size("gx")
    slab_rows = fields.shape[1]
    total_x = slab_rows * devices
    var_count = fields.shape[0]
    cells_y = fields.shape[2]
    cells_z = fields.shape[3]
    local_vars = jnp.einsum("vxyz,wxyz->vw", fields, fields, precision=highest)
    local_y = jnp.einsum("vxyz,vxuz->yu", fields, fields, precision=highest)
    flat = fields.reshape(-1, cells_z)
    local_z = jnp.dot(flat.T, flat, precision=highest, preferred_element_type=jnp.float32)
    summed_vars, summed_y, summed_z = lax.psum((local_vars, local_y, local_z), "gx")
    gram_vars = summed_vars / float(total_x * cells_y * cells_z)
    gram_y = summed_y / float(var_count * total_x * cells_z)
    gram_z = summed_z / float(var_count * total_x * cells_y)
    reduced_var = jnp.einsum("va,vxyz->axyz", factor_var, fields, precision=highest)
    reduced_z = jnp.einsum("axyz,zk->axyk", reduced_var, factor_z, precision=highest)
    reduced_y = jnp.einsum("axyk,yj->xajk", reduced_z, factor_y, precision=highest)
    comp_count = reduced_y.shape[1]
    projected = reduced_y.reshape(slab_rows, comp_count, reduced_y.shape[2] * reduced_y.shape[3])
    core_tensor = jnp.einsum(
        "xak,xr->kar",
        lax.all_to_all(projected, "gx", split_axis=2, concat_axis=0, tiled=True),
        factor_x,
        precision=highest,
    )
    return (core_tensor, gram_vars, gram_y, gram_z)


N = 16
V = 16
A = 8
S = 2
C = 256
R = 96
KP = 128
JD = R // N
CH = JD * S * A
GROUP = 4
TAIL = 24
PK = CH - TAIL
PIECE = 48


def split(value):
    high = value.astype(BF16)
    return high, (value - high.astype(F32)).astype(BF16)


def dot(a, b):
    return jnp.dot(a, b, preferred_element_type=F32)


def kernel(f_hbm, fy_ref, fz_ref, fv_ref, r_ref, gv_out, out,
           f_ref, h_ref, l_ref, zhl, yhl, pad, w_ref, p_ref, pk_ref, gy_acc, gz_acc, gv_acc,
           gram, recv_a, send_b, recv_b, send_c, recv_c, gv_all,
           s_load, s_core, r_core, s_gv, r_gv, s_a, r_a, s_b, r_b, s_c, r_c,
           s_cg, r_cg, s_bg, r_bg, s_ag, r_ag):
    me = lax.axis_index("gx")

    def load(i):
        x = i // (V // GROUP)
        first = lax.rem(i, V // GROUP) * GROUP
        part = pl.ds(first, GROUP)
        return pltpu.make_async_copy(f_hbm.at[part, x], f_ref.at[part, x], s_load.at[i])

    for i in range(S * V // GROUP):
        load(i).start()

    barrier = pltpu.get_barrier_semaphore()
    for off in range(1, N):
        pl.semaphore_signal(barrier, inc=1, device_id={"gx": lax.rem(me + off, N)}, device_id_type=MESH)

    def remote(src, dst, ssem, rsem, peer):
        return pltpu.make_async_remote_copy(
            src_ref=src, dst_ref=dst, send_sem=ssem, recv_sem=rsem,
            device_id={"gx": peer}, device_id_type=MESH)

    pad[...] = jnp.zeros((KP, C), F32)
    pad[0:R, :] = fz_ref[...]
    z_high, z_low = split(pad[...].T)
    zhl[:, 0:KP] = z_high
    zhl[:, KP:2 * KP] = z_low
    y_high, y_low = split(fy_ref[...])
    yhl[0:R, :] = y_high
    yhl[R:2 * R, :] = y_low

    def project(i, carry):
        x = i // (V // GROUP)
        first = lax.rem(i, V // GROUP) * GROUP
        load(i).wait()
        for u in range(GROUP):
            v = first + u
            high, low = split(f_ref[v, x])
            h_ref[v, x] = high
            l_ref[v, x] = low
            o = dot(yhl[...], jnp.concatenate([high, low], axis=1))
            along_y = o[0:R, 0:C] + (o[0:R, C:] + o[R:, 0:C])
            u_high, u_low = split(along_y)
            q = dot(jnp.concatenate([u_high, u_low], axis=0), zhl[...])
            w_ref[x * V + v] = q[0:R, 0:KP] + (q[0:R, KP:] + q[R:, 0:KP])
        return carry

    lax.fori_loop(0, S * V // GROUP, project, 0)

    for x in range(S):
        for a in range(A):
            total = fv_ref[a, 0] * w_ref[x * V]
            for v in range(1, V):
                total = total + fv_ref[a, v] * w_ref[x * V + v]
            p_ref[pl.ds(x * A + a, R, stride=S * A), :] = total

    lane = lax.broadcasted_iota(jnp.int32, (TAIL, KP), 1)
    for d in range(N):
        tail = p_ref[d * CH + PK:(d + 1) * CH, :]
        for t in range(3):
            rolled = pltpu.roll(tail, R - 32 * t, 1)
            pk_ref[d * PK + t * TAIL:d * PK + (t + 1) * TAIL, :] = jnp.where(
                lane >= R, rolled, p_ref[d * CH + t * TAIL:d * CH + (t + 1) * TAIL, :])

    pl.semaphore_wait(barrier, N - 1)

    q4 = lax.rem(me, 4)
    core = lax.rem(me, 2)
    xx = lax.rem(me // 2, 2)
    zz = me // 4
    pair = me + 1 - 2 * core
    xpair = me + 2 - 4 * xx

    def zpeer(off):
        return lax.rem(zz + off, 4)

    def chunk(index):
        return pl.ds(pl.multiple_of(index * PK, 8), PK)

    def core_copy(dz, dq):
        peer = zpeer(dz) * 4 + lax.rem(q4 + dq, 4)
        sem = dz * 4 + dq
        return remote(pk_ref.at[chunk(peer)], r_ref.at[chunk(me)], s_core.at[sem], r_core.at[sem], peer)

    others = [(dz, dq) for dz in (2, 1, 3, 0) for dq in range(4) if dz or dq]
    for dz, dq in others:
        core_copy(dz, dq).start()
    r_ref[chunk(me), :] = pk_ref[chunk(me), :]

    gy_acc[...] = jnp.zeros((2 * C, C), F32)
    gz_acc[...] = jnp.zeros((C, 2 * C), F32)
    gv_acc[...] = jnp.zeros((2 * C, C), F32)

    def grams(i, carry):
        x = i // (V // GROUP)
        first = lax.rem(i, V // GROUP) * GROUP
        highs = [h_ref[first + u, x] for u in range(GROUP)]
        lows = [l_ref[first + u, x] for u in range(GROUP)]
        turned = [h.T for h in highs]
        both = jnp.concatenate([jnp.concatenate(highs, axis=1), jnp.concatenate(lows, axis=1)], axis=0)
        gy_acc[...] += dot(both, jnp.concatenate(turned, axis=0))
        wide = jnp.concatenate([jnp.concatenate(highs, axis=0), jnp.concatenate(lows, axis=0)], axis=1)
        gz_acc[...] += dot(jnp.concatenate(turned, axis=1), wide)
        rows = [pl.ds(pl.multiple_of((first + u) * 16, 16), 16) for u in range(GROUP)]
        vh = jnp.concatenate([h_ref[:, x, r, :].reshape(C, C) for r in rows], axis=1)
        vl = jnp.concatenate([l_ref[:, x, r, :].reshape(C, C) for r in rows], axis=1)
        gv_acc[...] += lax.dot_general(
            jnp.concatenate([vh, vl], axis=0), vh, (((1,), (1,)), ((), ())), preferred_element_type=F32)
        return carry

    lax.fori_loop(0, S * V // GROUP, grams, 0)

    whole_y = gy_acc[0:C, :] + (gy_acc[C:, :] + gy_acc[C:, :].T)
    whole_z = gz_acc[:, 0:C] + (gz_acc[:, C:] + gz_acc[:, C:].T)
    for m, whole in enumerate((whole_y, whole_z)):
        gram[m * 384:m * 384 + 128, :] = whole[0:128, 0:128]
        gram[m * 384 + 128:m * 384 + 256, :] = whole[0:128, 128:]
        gram[m * 384 + 256:m * 384 + 384, :] = whole[128:, 128:]

    def piece(c, x, z):
        return pl.ds(pl.multiple_of(((c * 2 + x) * 4 + z) * PIECE, 8), PIECE)

    order = (1, 2, 3, 0)

    def a_copy(k, off):
        x = (1 - xx) if k == 0 else xx
        sem = k * 4 + off
        return remote(gram.at[piece(1 - core, x, zpeer(off))], recv_a.at[sem], s_a.at[sem], r_a.at[sem], pair)

    for k in range(2):
        for off in order:
            a_copy(k, off).start()

    row = lax.broadcasted_iota(jnp.int32, (C, C), 0)
    col = lax.broadcasted_iota(jnp.int32, (C, C), 1)
    whole = gv_acc[0:C, :] + (gv_acc[C:, :] + gv_acc[C:, :].T)
    kept = jnp.where(lax.rem(row, 16) == lax.rem(col, 16), whole, 0.0)
    pick_col = (lax.broadcasted_iota(jnp.int32, (C, KP), 0) // 16
                == lax.broadcasted_iota(jnp.int32, (C, KP), 1)).astype(F32)
    pick_row = (lax.broadcasted_iota(jnp.int32, (V, C), 1) // 16
                == lax.broadcasted_iota(jnp.int32, (V, C), 0)).astype(F32)
    highest = lax.Precision.HIGHEST
    by_col = jnp.dot(kept, pick_col, precision=highest, preferred_element_type=F32)
    by_both = jnp.dot(pick_row, by_col, precision=highest, preferred_element_type=F32)
    gv_all[me] = by_both[0:8, :] + pltpu.roll(by_both[8:16, :], 16, 1)

    def gv_copy(off):
        return remote(gv_all.at[me], gv_all.at[me], s_gv.at[off], r_gv.at[off], lax.rem(me + off, N))

    def b_copy(off):
        return remote(send_b.at[off], recv_b.at[off], s_b.at[off], r_b.at[off], xpair)

    def c_copy(off):
        return remote(send_c.at[off], recv_c.at[off], s_c.at[off], r_c.at[off], zpeer(off) * 4 + q4)

    for off in order:
        a_copy(0, off).wait()
        send_b[off] = gram[piece(core, 1 - xx, zpeer(off)), :] + recv_a[off]
        b_copy(off).start()
    for off in order:
        a_copy(1, off).wait()
        partial = gram[piece(core, xx, zpeer(off)), :] + recv_a[4 + off]
        b_copy(off).wait()
        send_c[off] = partial + recv_b[off]
        if off:
            c_copy(off).start()
    for off in range(1, N):
        gv_copy(off).start()
    mine = send_c[0]
    for off in range(1, 4):
        c_copy(off).wait()
        mine = mine + recv_c[off]
    out[piece(core, xx, zz), :] = mine * (1.0 / float(V * S * N * C))

    def cg_copy(off):
        at = piece(core, xx, zz)
        return remote(out.at[at], out.at[at], s_cg.at[off], r_cg.at[off], zpeer(off) * 4 + q4)

    def bg_copy(off):
        at = piece(core, xx, zpeer(4 - off))
        return remote(out.at[at], out.at[at], s_bg.at[off], r_bg.at[off], xpair)

    def ag_copy(k, off):
        at = piece(core, xx if k == 0 else 1 - xx, zpeer(4 - off))
        sem = k * 4 + off
        return remote(out.at[at], out.at[at], s_ag.at[sem], r_ag.at[sem], pair)

    for off in range(1, 4):
        cg_copy(off).start()
    for off in range(4):
        if off:
            cg_copy(off).wait()
        bg_copy(off).start()
        ag_copy(0, off).start()
    for off in range(4):
        bg_copy(off).wait()
        ag_copy(1, off).start()

    for off in range(1, N):
        gv_copy(off).wait()
    total = gv_all[0]
    for d in range(1, N):
        total = total + gv_all[d]
    gv_out[...] = total
    for dz, dq in others:
        core_copy(dz, dq).wait()
    for k in range(2):
        for off in range(4):
            ag_copy(k, off).wait()


def finish(r_ref, fx_ref, gram_ref, gv_ref, core_hbm, gv_out, gy_out, gz_out, un_ref, core_ref, sems):
    lane = lax.broadcasted_iota(jnp.int32, (TAIL, KP), 1)
    for d in range(N):
        parts = [r_ref[d * PK + t * TAIL:d * PK + (t + 1) * TAIL, :] for t in range(3)]
        for t in range(3):
            un_ref[d * CH + t * TAIL:d * CH + (t + 1) * TAIL, :] = parts[t]
        rolled = [pltpu.roll(parts[t], 32 * (t + 1), 1) for t in range(3)]
        un_ref[d * CH + PK:(d + 1) * CH, :] = jnp.where(
            lane < 32, rolled[0], jnp.where(lane < 64, rolled[1], rolled[2]))

    fx_high, fx_low = split(jnp.concatenate(
        [fx_ref[pl.ds(x, N, stride=S), :] for x in range(S)], axis=0))
    weights = jnp.concatenate([fx_high, fx_high, fx_low], axis=0).T
    copies = []
    for a in range(A):
        slabs = [jnp.concatenate(
            [un_ref[pl.ds(j * S * A + x * A + a, N, stride=CH), 0:R] for x in range(S)], axis=0)
            for j in range(JD)]
        high, low = split(jnp.concatenate(slabs, axis=1))
        core_ref[a] = dot(weights, jnp.concatenate([high, low, high], axis=0))
        copy = pltpu.make_async_copy(core_ref.at[a], core_hbm.at[a], sems.at[a])
        copy.start()
        copies.append(copy)

    scale = 1.0 / float(S * N * C * C)
    gv_out[0:8, :] = gv_ref[:, 0:V] * scale
    gv_out[8:16, :] = gv_ref[:, V:2 * V] * scale
    for m, o_ref in enumerate((gy_out, gz_out)):
        o_ref[0:128, 0:128] = gram_ref[m * 384:m * 384 + 128, :]
        off_block = gram_ref[m * 384 + 128:m * 384 + 256, :]
        o_ref[0:128, 128:] = off_block
        o_ref[128:, 0:128] = off_block.T
        o_ref[128:, 128:] = gram_ref[m * 384 + 256:m * 384 + 384, :]
    for copy in copies:
        copy.wait()


def fused(fields, factor_x, factor_y, factor_z, factor_var):
    vmem = pl.BlockSpec(memory_space=pltpu.VMEM)
    anywhere = pl.BlockSpec(memory_space=pl.ANY)
    dma = pltpu.SemaphoreType.DMA
    received, gv, gram = pl.pallas_call(
        kernel,
        out_shape=(
            jax.ShapeDtypeStruct((N * PK, KP), F32),
            jax.ShapeDtypeStruct((8, KP), F32),
            jax.ShapeDtypeStruct((16 * PIECE, 128), F32),
        ),
        in_specs=[anywhere, vmem, vmem, pl.BlockSpec(memory_space=pltpu.SMEM)],
        out_specs=(vmem, vmem, vmem),
        scratch_shapes=[
            pltpu.VMEM((V, S, C, C), F32),
            pltpu.VMEM((V, S, C, C), BF16), pltpu.VMEM((V, S, C, C), BF16),
            pltpu.VMEM((C, 2 * KP), BF16), pltpu.VMEM((2 * R, C), BF16), pltpu.VMEM((KP, C), F32),
            pltpu.VMEM((S * V, R, KP), F32),
            pltpu.VMEM((R * S * A, KP), F32), pltpu.VMEM((N * PK, KP), F32),
            pltpu.VMEM((2 * C, C), F32), pltpu.VMEM((C, 2 * C), F32), pltpu.VMEM((2 * C, C), F32),
            pltpu.VMEM((16 * PIECE, 128), F32), pltpu.VMEM((8, PIECE, 128), F32),
            pltpu.VMEM((4, PIECE, 128), F32), pltpu.VMEM((4, PIECE, 128), F32),
            pltpu.VMEM((4, PIECE, 128), F32), pltpu.VMEM((4, PIECE, 128), F32),
            pltpu.VMEM((N, 8, KP), F32),
            dma((S * V // GROUP,)), dma((N,)), dma((N,)), dma((N,)), dma((N,)),
            dma((8,)), dma((8,)), dma((4,)), dma((4,)), dma((4,)), dma((4,)),
            dma((4,)), dma((4,)), dma((4,)), dma((4,)), dma((8,)), dma((8,)),
        ],
        compiler_params=pltpu.CompilerParams(
            collective_id=0, has_side_effects=True, vmem_limit_bytes=56 * 1024 * 1024),
        name="fused",
    )(fields, factor_y.T, factor_z.T, factor_var.T)
    core, gram_v, gram_y, gram_z = pl.pallas_call(
        finish,
        out_shape=(
            jax.ShapeDtypeStruct((A, R, JD * R), F32),
            jax.ShapeDtypeStruct((V, V), F32),
            jax.ShapeDtypeStruct((C, C), F32),
            jax.ShapeDtypeStruct((C, C), F32),
        ),
        in_specs=[vmem] * 4,
        out_specs=(anywhere, vmem, vmem, vmem),
        scratch_shapes=[pltpu.VMEM((N * CH, KP), F32), pltpu.VMEM((A, R, JD * R), F32), dma((A,))],
        compiler_params=pltpu.CompilerParams(vmem_limit_bytes=32 * 1024 * 1024),
        name="finish",
    )(received, factor_x, gram, gv)
    return core.transpose(2, 0, 1), gram_v, gram_y, gram_z


def local(fields, factor_x, factor_y, factor_z, factor_var):
    sizes = (fields.shape, factor_x.shape, factor_y.shape, factor_z.shape, factor_var.shape)
    served = ((V, S, C, C), (S * N, R), (C, R), (C, R), (V, A))
    if lax.axis_size("gx") == N and sizes == served:
        return fused(fields, factor_x, factor_y, factor_z, factor_var)
    return plain(fields, factor_x, factor_y, factor_z, factor_var)


def solution(mesh):
    in_specs = (
        P("grp", "gx", None, None),
        P("grp", None),
        P("grp", None),
        P("grp", None),
        P("grp", None),
    )
    out_specs = (P(("grp", "gx"), None, None), P("grp", None), P("grp", None), P("grp", None))
    return jax.shard_map(local, mesh=mesh, in_specs=in_specs, out_specs=out_specs, check_vma=False)
```

time: 62.2 us -> 49.7 us (0.80)
  local copies, waits for them, and re-layouts: 9.96 us -> 2.73 us
  Pallas kernels: 51.3 us -> 46 us
    unnamed x13 -> x8, local copies, waits for them, and re-layouts: 9.96 us -> 2.73 us
    pallas_call x1 -> x2, Pallas kernels: 51.3 us -> 46 us  [the longest x1 43.3 us: fused(): pl.pallas_call(kernel, out_shape=(jax.ShapeDtypeStruct((N * PK, KP), F32)...]
where the time goes in v1:
time: 49.7 us; the launch traced here: 49.4 us
  Pallas kernels  46 us (93%)
  local copies, waits for them, and re-layouts  2.73 us (5%)
  between operations  0.67 us (1%)
    pallas_call x1, Pallas kernels, fused(): pl.pallas_call(kernel, out_shape=(jax.ShapeDtypeStruct((N * PK, KP), F32)...  43.3 us
    unnamed x8, local copies, waits for them, and re-layouts  2.73 us
    pallas_call x1, Pallas kernels, fused(): pl.pallas_call(finish, out_shape=(jax.ShapeDtypeStruct((A, R, JD * R), F3...  2.72 us

profile of v1, /device:TPU:0, one launch (start us, length us, event | category | flops | bytes accessed | tf_op | source)
XLA Modules:
  0.0 49.4 jit_solution(15957745935366689219)
XLA Ops:
  0.6 0.0 copy-start.2
  0.6 43.3 %fused.1 = (f32[1152,128]{1,0:T(8,128)}, f32[8,128]{1,0:T(8,128)}, f32[768,128]{1,0:T(8,128)}) custom-call(f32[16,2,256,256]{3,2,1,0:T(8,128)} %f_hbm.1, f32[96,256]{1,0:T(8,128)} %bitcast.4, f32[96,256]{1,0:T(8,128)} %bitcast.5, f32[8,16]{1,0:T(8,128)} %bitcast.6), custom_call_target="tpu_custom_call" | custom-call | tf_op jit(solution)/shard_map/fused/pallas_call | solution.py:322
  43.9 0.0 copy-done.2
  44.0 0.0 copy-start
  44.0 1.1 %copy-done = f32[1152,128]{1,0:T(8,128)S(1)} copy-done((f32[1152,128]{1,0:T(8,128)S(1)}, f32[1152,128]{1,0:T(8,128)}, u32[]{:S(2)}) %copy-start) | copy-done | bytes 589848
  45.0 0.0 copy-start.1
  45.0 1.0 %copy-done.1 = f32[768,128]{1,0:T(8,128)S(1)} copy-done((f32[768,128]{1,0:T(8,128)S(1)}, f32[768,128]{1,0:T(8,128)}, u32[]{:S(2)}) %copy-start.1) | copy-done | bytes 393240
  46.0 0.0 copy-start.3
  46.0 0.7 %copy-done.3 = f32[8,128]{1,0:T(8,128)S(1)} copy-done((f32[8,128]{1,0:T(8,128)S(1)}, f32[8,128]{1,0:T(8,128)}, u32[]{:S(2)}) %copy-start.3) | copy-done | bytes 4120
  46.7 2.7 %finish.1 = (f32[8,96,576]{2,1,0:T(8,128)}, f32[16,16]{1,0:T(8,128)}, f32[256,256]{1,0:T(8,128)}, f32[256,256]{1,0:T(8,128)}) custom-call(f32[1152,128]{1,0:T(8,128)S(1)} %copy-done, f32[32,96]{1,0:T(8,128)S(1)} %copy-done.2, f32[768,128]{1,0:T(8,128)S(1)} %copy-done.1, f32[8,128]{1,0:T(8,128)S(1)} %copy-done.3), custom_call_target="tpu_custom_call" | custom-call | tf_op jit(solution)/shard_map/finish/pallas_call | solution.py:350
Async XLA Ops:
  0.6 43.3 %copy-start.2 = (f32[32,96]{1,0:T(8,128)S(1)}, f32[32,96]{1,0:T(8,128)}, u32[]{:S(2)}) copy-start(f32[32,96]{1,0:T(8,128)} %fx_ref.1) | copy-start | bytes 36868
  44.0 1.1 %copy-start = (f32[1152,128]{1,0:T(8,128)S(1)}, f32[1152,128]{1,0:T(8,128)}, u32[]{:S(2)}) copy-start(f32[1152,128]{1,0:T(8,128)} %get-tuple-element.11.r_ref) | copy-start | bytes 1769476
  45.0 1.0 %copy-start.1 = (f32[768,128]{1,0:T(8,128)S(1)}, f32[768,128]{1,0:T(8,128)}, u32[]{:S(2)}) copy-start(f32[768,128]{1,0:T(8,128)} %get-tuple-element.12.gram_ref) | copy-start | bytes 1179652
  46.0 0.7 %copy-start.3 = (f32[8,128]{1,0:T(8,128)S(1)}, f32[8,128]{1,0:T(8,128)}, u32[]{:S(2)}) copy-start(f32[8,128]{1,0:T(8,128)} %get-tuple-element.13.gv_ref) | copy-start | bytes 12292

commit v2 on v1

--- a/solution.py
+++ b/solution.py
@@ -170,6 +170,13 @@
         gy_acc[...] += dot(both, jnp.concatenate(turned, axis=0))
         wide = jnp.concatenate([jnp.concatenate(highs, axis=0), jnp.concatenate(lows, axis=0)], axis=1)
         gz_acc[...] += dot(jnp.concatenate(turned, axis=1), wide)
+        return carry
+
+    lax.fori_loop(0, S * V // GROUP, grams, 0)
+
+    def gram_v(i, carry):
+        x = i // (V // GROUP)
+        first = lax.rem(i, V // GROUP) * GROUP
         rows = [pl.ds(pl.multiple_of((first + u) * 16, 16), 16) for u in range(GROUP)]
         vh = jnp.concatenate([h_ref[:, x, r, :].reshape(C, C) for r in rows], axis=1)
         vl = jnp.concatenate([l_ref[:, x, r, :].reshape(C, C) for r in rows], axis=1)
@@ -177,8 +184,6 @@
             jnp.concatenate([vh, vl], axis=0), vh, (((1,), (1,)), ((), ())), preferred_element_type=F32)
         return carry
 
-    lax.fori_loop(0, S * V // GROUP, grams, 0)
-
     whole_y = gy_acc[0:C, :] + (gy_acc[C:, :] + gy_acc[C:, :].T)
     whole_z = gz_acc[:, 0:C] + (gz_acc[:, C:] + gz_acc[:, C:].T)
     for m, whole in enumerate((whole_y, whole_z)):
@@ -200,6 +205,30 @@
         for off in order:
             a_copy(k, off).start()
 
+    lax.fori_loop(0, V // GROUP, gram_v, 0)
+
+    def gv_copy(off):
+        return remote(gv_all.at[me], gv_all.at[me], s_gv.at[off], r_gv.at[off], lax.rem(me + off, N))
+
+    def b_copy(off):
+        return remote(send_b.at[off], recv_b.at[off], s_b.at[off], r_b.at[off], xpair)
+
+    def c_copy(off):
+        return remote(send_c.at[off], recv_c.at[off], s_c.at[off], r_c.at[off], zpeer(off) * 4 + q4)
+
+    for off in order:
+        a_copy(0, off).wait()
+        send_b[off] = gram[piece(core, 1 - xx, zpeer(off)), :] + recv_a[off]
+        b_copy(off).start()
+
+    lax.fori_loop(V // GROUP, S * V // GROUP, gram_v, 0)
+    for off in order:
+        a_copy(1, off).wait()
+        partial = gram[piece(core, xx, zpeer(off)), :] + recv_a[4 + off]
+        b_copy(off).wait()
+        send_c[off] = partial + recv_b[off]
+        if off:
+            c_copy(off).start()
     row = lax.broadcasted_iota(jnp.int32, (C, C), 0)
     col = lax.broadcasted_iota(jnp.int32, (C, C), 1)
     whole = gv_acc[0:C, :] + (gv_acc[C:, :] + gv_acc[C:, :].T)
@@ -213,26 +242,6 @@
     by_both = jnp.dot(pick_row, by_col, precision=highest, preferred_element_type=F32)
     gv_all[me] = by_both[0:8, :] + pltpu.roll(by_both[8:16, :], 16, 1)
 
-    def gv_copy(off):
-        return remote(gv_all.at[me], gv_all.at[me], s_gv.at[off], r_gv.at[off], lax.rem(me + off, N))
-
-    def b_copy(off):
-        return remote(send_b.at[off], recv_b.at[off], s_b.at[off], r_b.at[off], xpair)
-
-    def c_copy(off):
-        return remote(send_c.at[off], recv_c.at[off], s_c.at[off], r_c.at[off], zpeer(off) * 4 + q4)
-
-    for off in order:
-        a_copy(0, off).wait()
-        send_b[off] = gram[piece(core, 1 - xx, zpeer(off)), :] + recv_a[off]
-        b_copy(off).start()
-    for off in order:
-        a_copy(1, off).wait()
-        partial = gram[piece(core, xx, zpeer(off)), :] + recv_a[4 + off]
-        b_copy(off).wait()
-        send_c[off] = partial + recv_b[off]
-        if off:
-            c_copy(off).start()
     for off in range(1, N):
         gv_copy(off).start()
     mine = send_c[0]
@@ -278,7 +287,14 @@
             ag_copy(k, off).wait()
 
 
-def finish(r_ref, fx_ref, gram_ref, gv_ref, core_hbm, gv_out, gy_out, gz_out, un_ref, core_ref, sems):
+def finish(r_hbm, fx_ref, gram_hbm, gv_hbm, core_hbm, gv_out, gy_out, gz_out,
+           r_ref, gram_ref, gv_ref, un_ref, core_ref, s_in, sems):
+    loads = [pltpu.make_async_copy(src, dst, s_in.at[i]) for i, (src, dst) in enumerate(
+        ((r_hbm, r_ref), (gram_hbm, gram_ref), (gv_hbm, gv_ref)))]
+    for load in loads:
+        load.start()
+    loads[0].wait()
+
     lane = lax.broadcasted_iota(jnp.int32, (TAIL, KP), 1)
     for d in range(N):
         parts = [r_ref[d * PK + t * TAIL:d * PK + (t + 1) * TAIL, :] for t in range(3)]
@@ -302,6 +318,8 @@
         copy.start()
         copies.append(copy)
 
+    loads[1].wait()
+    loads[2].wait()
     scale = 1.0 / float(S * N * C * C)
     gv_out[0:8, :] = gv_ref[:, 0:V] * scale
     gv_out[8:16, :] = gv_ref[:, V:2 * V] * scale
@@ -318,6 +336,7 @@
 def fused(fields, factor_x, factor_y, factor_z, factor_var):
     vmem = pl.BlockSpec(memory_space=pltpu.VMEM)
     anywhere = pl.BlockSpec(memory_space=pl.ANY)
+    in_hbm = pl.BlockSpec(memory_space=pltpu.HBM)
     dma = pltpu.SemaphoreType.DMA
     received, gv, gram = pl.pallas_call(
         kernel,
@@ -355,10 +374,12 @@
             jax.ShapeDtypeStruct((C, C), F32),
             jax.ShapeDtypeStruct((C, C), F32),
         ),
-        in_specs=[vmem] * 4,
+        in_specs=[in_hbm, vmem, in_hbm, in_hbm],
         out_specs=(anywhere, vmem, vmem, vmem),
-        scratch_shapes=[pltpu.VMEM((N * CH, KP), F32), pltpu.VMEM((A, R, JD * R), F32), dma((A,))],
-        compiler_params=pltpu.CompilerParams(vmem_limit_bytes=32 * 1024 * 1024),
+        scratch_shapes=[
+            pltpu.VMEM((N * PK, KP), F32), pltpu.VMEM((16 * PIECE, 128), F32), pltpu.VMEM((8, KP), F32),
+            pltpu.VMEM((N * CH, KP), F32), pltpu.VMEM((A, R, JD * R), F32), dma((3,)), dma((A,))],
+        compiler_params=pltpu.CompilerParams(vmem_limit_bytes=60 * 1024 * 1024),
         name="finish",
     )(received, factor_x, gram, gv)
     return core.transpose(2, 0, 1), gram_v, gram_y, gram_z

time: 49.7 us -> 48.2 us (0.970)
  local copies, waits for them, and re-layouts: 2.73 us -> 0 us
  Pallas kernels: 46 us -> 47.3 us
    unnamed x8 -> x0, local copies, waits for them, and re-layouts: 2.73 us -> none
    pallas_call x1, Pallas kernels: 2.72 us -> 4.53 us  [fused(): pl.pallas_call(finish, out_shape=(jax.ShapeDtypeStruct((A, R, JD * R), F3...]
    pallas_call x1, Pallas kernels: 43.3 us -> 42.8 us  [fused(): pl.pallas_call(kernel, out_shape=(jax.ShapeDtypeStruct((N * PK, KP), F32)...]
where the time goes in v2:
time: 48.2 us; the launch traced here: 48 us
  Pallas kernels  47.3 us (98%)
  between operations  0.64 us (1%)
    pallas_call x1, Pallas kernels, fused(): pl.pallas_call(kernel, out_shape=(jax.ShapeDtypeStruct((N * PK, KP), F32)...  42.8 us
    pallas_call x1, Pallas kernels, fused(): pl.pallas_call(finish, out_shape=(jax.ShapeDtypeStruct((A, R, JD * R), F3...  4.53 us

profile of v2, /device:TPU:0, one launch (start us, length us, event | category | flops | bytes accessed | tf_op | source)
XLA Modules:
  0.0 48.0 jit_solution(14248798134176007441)
XLA Ops:
  0.6 42.8 %fused.1 = (f32[1152,128]{1,0:T(8,128)}, f32[8,128]{1,0:T(8,128)}, f32[768,128]{1,0:T(8,128)}) custom-call(f32[16,2,256,256]{3,2,1,0:T(8,128)} %f_hbm.1, f32[96,256]{1,0:T(8,128)} %bitcast.4, f32[96,256]{1,0:T(8,128)} %bitcast.5, f32[8,16]{1,0:T(8,128)} %bitcast.6), custom_call_target="tpu_custom_call" | custom-call | tf_op jit(solution)/shard_map/fused/pallas_call | solution.py:341
  43.4 4.5 %finish.1 = (f32[8,96,576]{2,1,0:T(8,128)}, f32[16,16]{1,0:T(8,128)}, f32[256,256]{1,0:T(8,128)}, f32[256,256]{1,0:T(8,128)}) custom-call(f32[1152,128]{1,0:T(8,128)} %get-tuple-element.11.r_hbm, f32[32,96]{1,0:T(8,128)} %fx_ref.1, f32[768,128]{1,0:T(8,128)} %get-tuple-element.12.gram_hbm, f32[8,128]{1,0:T(8,128)} %get-tuple-element.13.gv_hbm), custom_call_target="tpu_custom_call" | custom-call | tf_op jit(solution)/shard_map/finish/pallas_call | solution.py:369

commit v3 on v2

--- a/solution.py
+++ b/solution.py
@@ -101,12 +101,9 @@
     def project(i, carry):
         x = i // (V // GROUP)
         first = lax.rem(i, V // GROUP) * GROUP
-        load(i).wait()
         for u in range(GROUP):
             v = first + u
-            high, low = split(f_ref[v, x])
-            h_ref[v, x] = high
-            l_ref[v, x] = low
+            high, low = h_ref[v, x], l_ref[v, x]
             o = dot(yhl[...], jnp.concatenate([high, low], axis=1))
             along_y = o[0:R, 0:C] + (o[0:R, C:] + o[R:, 0:C])
             u_high, u_low = split(along_y)
@@ -114,23 +111,6 @@
             w_ref[x * V + v] = q[0:R, 0:KP] + (q[0:R, KP:] + q[R:, 0:KP])
         return carry
 
-    lax.fori_loop(0, S * V // GROUP, project, 0)
-
-    for x in range(S):
-        for a in range(A):
-            total = fv_ref[a, 0] * w_ref[x * V]
-            for v in range(1, V):
-                total = total + fv_ref[a, v] * w_ref[x * V + v]
-            p_ref[pl.ds(x * A + a, R, stride=S * A), :] = total
-
-    lane = lax.broadcasted_iota(jnp.int32, (TAIL, KP), 1)
-    for d in range(N):
-        tail = p_ref[d * CH + PK:(d + 1) * CH, :]
-        for t in range(3):
-            rolled = pltpu.roll(tail, R - 32 * t, 1)
-            pk_ref[d * PK + t * TAIL:d * PK + (t + 1) * TAIL, :] = jnp.where(
-                lane >= R, rolled, p_ref[d * CH + t * TAIL:d * CH + (t + 1) * TAIL, :])
-
     pl.semaphore_wait(barrier, N - 1)
 
     q4 = lax.rem(me, 4)
@@ -151,11 +131,6 @@
         sem = dz * 4 + dq
         return remote(pk_ref.at[chunk(peer)], r_ref.at[chunk(me)], s_core.at[sem], r_core.at[sem], peer)
 
-    others = [(dz, dq) for dz in (2, 1, 3, 0) for dq in range(4) if dz or dq]
-    for dz, dq in others:
-        core_copy(dz, dq).start()
-    r_ref[chunk(me), :] = pk_ref[chunk(me), :]
-
     gy_acc[...] = jnp.zeros((2 * C, C), F32)
     gz_acc[...] = jnp.zeros((C, 2 * C), F32)
     gv_acc[...] = jnp.zeros((2 * C, C), F32)
@@ -163,8 +138,13 @@
     def grams(i, carry):
         x = i // (V // GROUP)
         first = lax.rem(i, V // GROUP) * GROUP
-        highs = [h_ref[first + u, x] for u in range(GROUP)]
-        lows = [l_ref[first + u, x] for u in range(GROUP)]
+        load(i).wait()
+        parts = [split(f_ref[first + u, x]) for u in range(GROUP)]
+        highs = [high for high, low in parts]
+        lows = [low for high, low in parts]
+        for u in range(GROUP):
+            h_ref[first + u, x] = highs[u]
+            l_ref[first + u, x] = lows[u]
         turned = [h.T for h in highs]
         both = jnp.concatenate([jnp.concatenate(highs, axis=1), jnp.concatenate(lows, axis=1)], axis=0)
         gy_acc[...] += dot(both, jnp.concatenate(turned, axis=0))
@@ -205,7 +185,7 @@
         for off in order:
             a_copy(k, off).start()
 
-    lax.fori_loop(0, V // GROUP, gram_v, 0)
+    lax.fori_loop(0, V // GROUP, project, 0)
 
     def gv_copy(off):
         return remote(gv_all.at[me], gv_all.at[me], s_gv.at[off], r_gv.at[off], lax.rem(me + off, N))
@@ -221,7 +201,23 @@
         send_b[off] = gram[piece(core, 1 - xx, zpeer(off)), :] + recv_a[off]
         b_copy(off).start()
 
-    lax.fori_loop(V // GROUP, S * V // GROUP, gram_v, 0)
+    lax.fori_loop(V // GROUP, S * V // GROUP, project, 0)
+
+    for x in range(S):
+        for a in range(A):
+            total = fv_ref[a, 0] * w_ref[x * V]
+            for v in range(1, V):
+                total = total + fv_ref[a, v] * w_ref[x * V + v]
+            p_ref[pl.ds(x * A + a, R, stride=S * A), :] = total
+
+    lane = lax.broadcasted_iota(jnp.int32, (TAIL, KP), 1)
+    for d in range(N):
+        tail = p_ref[d * CH + PK:(d + 1) * CH, :]
+        for t in range(3):
+            rolled = pltpu.roll(tail, R - 32 * t, 1)
+            pk_ref[d * PK + t * TAIL:d * PK + (t + 1) * TAIL, :] = jnp.where(
+                lane >= R, rolled, p_ref[d * CH + t * TAIL:d * CH + (t + 1) * TAIL, :])
+
     for off in order:
         a_copy(1, off).wait()
         partial = gram[piece(core, xx, zpeer(off)), :] + recv_a[4 + off]
@@ -229,6 +225,13 @@
         send_c[off] = partial + recv_b[off]
         if off:
             c_copy(off).start()
+
+    others = [(dz, dq) for dz in (2, 1, 3, 0) for dq in range(4) if dz or dq]
+    for dz, dq in others:
+        core_copy(dz, dq).start()
+    r_ref[chunk(me), :] = pk_ref[chunk(me), :]
+
+    lax.fori_loop(0, S * V // GROUP, gram_v, 0)
     row = lax.broadcasted_iota(jnp.int32, (C, C), 0)
     col = lax.broadcasted_iota(jnp.int32, (C, C), 1)
     whole = gv_acc[0:C, :] + (gv_acc[C:, :] + gv_acc[C:, :].T)

time: 48.2 us -> 54.6 us (1.13)
  Pallas kernels: 47.3 us -> 53.7 us
    pallas_call x1, Pallas kernels: 42.8 us -> 49.2 us  [fused(): pl.pallas_call(kernel, out_shape=(jax.ShapeDtypeStruct((N * PK, KP), F32)...]
where the time goes in v3:
time: 54.6 us; the launch traced here: 54.3 us
  Pallas kernels  53.7 us (98%)
  between operations  0.64 us (1%)
    pallas_call x1, Pallas kernels, fused(): pl.pallas_call(kernel, out_shape=(jax.ShapeDtypeStruct((N * PK, KP), F32)...  49.2 us
    pallas_call x1, Pallas kernels, fused(): pl.pallas_call(finish, out_shape=(jax.ShapeDtypeStruct((A, R, JD * R), F3...  4.53 us

profile of v3, /device:TPU:0, one launch (start us, length us, event | category | flops | bytes accessed | tf_op | source)
XLA Modules:
  0.0 54.3 jit_solution(14350377857019843089)
XLA Ops:
  0.6 49.2 %fused.1 = (f32[1152,128]{1,0:T(8,128)}, f32[8,128]{1,0:T(8,128)}, f32[768,128]{1,0:T(8,128)}) custom-call(f32[16,2,256,256]{3,2,1,0:T(8,128)} %f_hbm.1, f32[96,256]{1,0:T(8,128)} %bitcast.4, f32[96,256]{1,0:T(8,128)} %bitcast.5, f32[8,16]{1,0:T(8,128)} %bitcast.6), custom_call_target="tpu_custom_call" | custom-call | tf_op jit(solution)/shard_map/fused/pallas_call | solution.py:344
  49.8 4.5 %finish.1 = (f32[8,96,576]{2,1,0:T(8,128)}, f32[16,16]{1,0:T(8,128)}, f32[256,256]{1,0:T(8,128)}, f32[256,256]{1,0:T(8,128)}) custom-call(f32[1152,128]{1,0:T(8,128)} %get-tuple-element.11.r_hbm, f32[32,96]{1,0:T(8,128)} %fx_ref.1, f32[768,128]{1,0:T(8,128)} %get-tuple-element.12.gram_hbm, f32[8,128]{1,0:T(8,128)} %get-tuple-element.13.gv_hbm), custom_call_target="tpu_custom_call" | custom-call | tf_op jit(solution)/shard_map/finish/pallas_call | solution.py:372
